TPU v7x, 512 devices: a whole 4x4x16 slice. The times are simulated.
512 devices in a mesh: feat: 64 (over z_lo, y, core), tok: 8 (over z_hi, x).
Axes of the slice: x: 4, y: 4, z: 16 (z_hi: 2, z_lo: 8; z = z_hi * 8 + z_lo), core: 2. Of those that a mesh axis runs over, the one named last changes fastest.
Arguments:
- source: bfloat16 [1024, 3584], P(('tok', 'feat')), may hold values from -6 to 6
- target: bfloat16 [1024, 3584], P(('tok', 'feat')), may hold values from -6 to 6
- enc_weight: bfloat16 [3584, 16384], P('tok', 'feat'), may hold values from -0.09375 to 0.09375
- enc_bias: float32 [16384], P('feat'), may hold values from -3 to 3
- dec_weight: bfloat16 [16384, 3584], P('feat', 'tok'), may hold values from -0.09375 to 0.09375
- active: int32 [1024, 16384], P('tok', 'feat'), may hold values 0 or 1
Outputs:
- recon_error: float32 [1024, 3584], P(('tok', 'feat'))
- grad_enc: bfloat16 [3584, 16384], P(None, 'feat')
- grad_bias: float32 [16384], P('feat')
- grad_dec: bfloat16 [16384, 3584], P('feat')
All inputs are finite; a program needn't handle non-finite values. No bound on the sum of `active` on one device may be relied on, other than what follows from the above.
Results may differ from a plain program's by a relative error of at most 0.019.
Values may be sent and summed in bfloat16 or wider, within the bound.
A program may use at most 64 MiB of HBM per device.

v0:
```python
import math
import jax
import jax.numpy as jnp
from jax import lax
from jax.sharding import PartitionSpec as P


def on_device(source, target, enc_weight, enc_bias, dec_weight, active):
    row_count = source.shape[0]
    group_rows = row_count * lax.axis_size("feat")
    token_total = group_rows * lax.axis_size("tok")
    gathered = lax.all_gather(source, "feat", axis=0, tiled=True)
    slab_rows = gathered
    preact = (
        jnp.dot(
            slab_rows,
            lax.all_gather(enc_weight, "tok", axis=0, tiled=True),
            preferred_element_type=jnp.float32,
        )
        + enc_bias
    )
    gating = active.astype(jnp.float32)
    features = (gating * preact).astype(jnp.bfloat16)
    full_dec = lax.all_gather(dec_weight, "tok", axis=1, tiled=True)
    slab_rows = features
    recon = lax.psum_scatter(
        jnp.dot(slab_rows, full_dec, preferred_element_type=jnp.float32),
        "feat",
        scatter_dimension=0,
        tiled=True,
    )
    recon_error = recon - target.astype(jnp.float32)
    signal = (recon_error * (1.0 / math.sqrt(token_total))).astype(jnp.bfloat16)
    signal_all = lax.all_gather(signal, "feat", axis=0, tiled=True)
    dec_part = lax.dot_general(
        features, signal_all, (((0,), (0,)), ((), ())), preferred_element_type=jnp.float32
    )
    backflow = lax.dot_general(
        signal_all, full_dec, (((1,), (1,)), ((), ())), preferred_element_type=jnp.float32
    )
    pre_grad = gating * backflow
    pre_round = pre_grad.astype(jnp.bfloat16)
    bias_part = jnp.sum(pre_grad, axis=0).astype(jnp.bfloat16)
    enc_part = lax.dot_general(
        gathered, pre_round, (((0,), (0,)), ((), ())), preferred_element_type=jnp.float32
    )
    enc_half = enc_part.astype(jnp.bfloat16)
    dec_half = dec_part.astype(jnp.bfloat16)
    enc_summed, dec_summed, bias_summed = (
        lax.psum(enc_half, "tok").astype(jnp.float32),
        lax.psum(dec_half, "tok").astype(jnp.float32),
        lax.psum(bias_part, "tok").astype(jnp.float32),
    )
    enc_out = enc_summed.astype(jnp.bfloat16)
    dec_out = dec_summed.astype(jnp.bfloat16)
    return (recon_error, enc_out, bias_summed, dec_out)


def solution(mesh):
    placed = (
        P(("tok", "feat"), None),
        P(("tok", "feat"), None),
        P("tok", "feat"),
        P("feat"),
        P("feat", "tok"),
        P("tok", "feat"),
    )
    return jax.shard_map(
        on_device,
        mesh=mesh,
        in_specs=placed,
        out_specs=(P(("tok", "feat"), None), P(None, "feat"), P("feat"), P("feat", None)),
        check_vma=False,
    )
```

profile of v0, /device:TPU:14, one launch (start us, length us, event | category | flops | bytes accessed | tf_op | source)
XLA Modules:
  0.0 1527.0 jit_solution(12357005956135973958)
XLA Ops:
  7.2 0.0 copy-start.2
  7.2 0.0 copy-start.4
  7.2 0.0 all-gather.5.cloned.1.call-start
  7.2 0.7 all-gather.5.cloned.1.call-update
  7.9 0.0 all-gather.7.cloned.1.call-start
  8.0 0.7 all-gather.7.cloned.1.call-update
  8.7 0.0 all-reduce.5.cloned.1.call-start
  8.7 148.6 %all-gather = bf16[64,2,3584]{2,1,0:T(2,128)(2,1)S(1)} all-gather(bf16[1,2,3584]{2,1,0:T(2,128)(2,1)} %bitcast.16), channel_id=1, replica_groups=mesh['feat'=64,'tok'=8] {'feat'}, dimensions={0}, use_global_device_ids=true | all-gather | bytes 931840 | tf_op jit(solution)/shard_map/all_gather | solution.py:12
  157.3 0.3 reshape.10
  157.7 0.0 all-gather.5.cloned.1.call-done
  157.7 0.0 copy-done.2
  157.7 0.0 copy-done.4
  157.7 1.9 fusion.2
  159.7 75.7 %all-gather.7.cloned.1.call-done = bf16[256,3584]{0,1:T(8,128)(2,1)} async-done(((bf16[256,448]{0,1:T(8,128)(2,1)}), bf16[256,3584]{0,1:T(8,128)(2,1)}) %all-gather.7.cloned.1.call-update) | async-done | bytes 1835024 | tf_op jit(solution)/shard_map/all_gather | solution.py:24
  235.3 3.5 fusion.6
  238.8 0.0 copy-start.3
  238.8 0.0 all-reduce.5.cloned.1.call-update
  238.8 0.0 all-reduce.7.cloned.1.call-start
  238.9 1.3 dynamic-slice
  240.8 810.8 %all-reduce.5.cloned.1.call-done = f32[128,3584]{1,0:T(8,128)} async-done(((f32[128,3584]{1,0:T(8,128)}), f32[128,3584]{1,0:T(8,128)}) %all-reduce.5.cloned.1.call-update) | async-done | bytes 1835024
  1051.6 0.0 copy-done.3
  1051.6 1.5 fusion.4
  1053.1 116.8 %all-gather.1 = bf16[64,2,3584]{2,1,0:T(2,128)(2,1)S(1)} all-gather(bf16[1,2,3584]{2,1,0:T(2,128)(2,1)S(1)} %get-tuple-element.14), channel_id=1, replica_groups=mesh['feat'=64,'tok'=8] {'feat'}, dimensions={0}, use_global_device_ids=true | all-gather | bytes 931840 | tf_op jit(solution)/shard_map/all_gather | solution.py:34
  1169.9 0.3 reshape.12
  1170.3 0.0 copy-start
  1170.3 1.9 convolution_convert_fusion
  1172.2 0.0 copy-done
  1172.2 0.4 fusion.5
  1172.6 1.9 fusion
  1174.5 0.0 all-reduce.7.cloned.1.call-update
  1174.5 39.5 %psum.22 = bf16[256]{0:T(256)(128)(2,1)S(1)} all-reduce(bf16[256]{0:T(256)(128)(2,1)S(1)} %get-tuple-element.16), channel_id=1, replica_groups=mesh['feat'=64,'tok'=8] {'tok'}, use_global_device_ids=true, to_apply=%region_3.0 | all-reduce | flops 256 | bytes 1024 | tf_op jit(solution)/shard_map/psum | solution.py:52
  1214.1 0.6 convert_element_type.42
  1214.6 300.7 %all-reduce.7.cloned.1.call-done = (bf16[3584,256]{0,1:T(8,128)(2,1)}, bf16[256,3584]{1,0:T(8,128)(2,1)}) async-done(((bf16[3584,256]{0,1:T(8,128)(2,1)}, bf16[256,3584]{1,0:T(8,128)(2,1)}), (bf16[3584,256]{0,1:T(8,128)(2,1)}, bf16[256,3584]{1,0:T(8,128)(2,1)})) %all-reduce.7.cloned.1.call-update) | async-done | bytes 3670032 | tf_op jit(solution)/shard_map/psum | solution.py:50
  1515.3 0.0 copy-start.1
  1515.3 3.9 copy.11
  1519.2 0.0 copy-done.1
  1519.3 1.2 copy.15
Async XLA Ops:
  7.2 150.6 %copy-start.2 = (s32[128,256]{1,0:T(8,128)S(1)}, s32[128,256]{1,0:T(8,128)}, u32[]{:S(2)}) copy-start(s32[128,256]{1,0:T(8,128)} %param.11) | copy-start | bytes 393220
  7.2 150.6 %copy-start.4 = (f32[256]{0:T(256)S(1)}, f32[256]{0:T(256)}, u32[]{:S(2)}) copy-start(f32[256]{0:T(256)} %param.9) | copy-start | bytes 3076
  7.2 150.5 %all-gather.5.cloned.1.call-start = ((), (), s32[]{:S(2)}) async-start(), calls=%async_computation | async-start | bytes 2064384 | tf_op jit(solution)/shard_map/all_gather | solution.py:17
  7.9 227.4 %all-gather.7.cloned.1.call-start = ((), (), s32[]{:S(2)}) async-start(), calls=%async_computation.1 | async-start | bytes 2064384 | tf_op jit(solution)/shard_map/all_gather | solution.py:24
  8.7 1042.9 %all-reduce.5.cloned.1.call-start = ((), (), s32[]{:S(2)}) async-start(), calls=%async_computation.2 | async-start | bytes 3670016
  238.8 812.8 %copy-start.3 = (bf16[2,3584]{1,0:T(2,128)(2,1)S(1)}, bf16[2,3584]{1,0:T(2,128)(2,1)}, u32[]{:S(2)}) copy-start(bf16[2,3584]{1,0:T(2,128)(2,1)} %param.7) | copy-start | bytes 43012
  238.8 1276.5 %all-reduce.7.cloned.1.call-start = ((), (), s32[]{:S(2)}) async-start(), calls=%async_computation.3 | async-start | bytes 7340032 | tf_op jit(solution)/shard_map/psum | solution.py:50
  1170.3 1.9 copy-start
  1515.3 3.9 copy-start.1
Sparse Core Ops, SparseCore 0:
  11.2 116.1 all-gather.4
  130.5 104.7 all-gather.6
  238.9 812.6 all-reduce.4
  1174.7 340.6 all-reduce.6
where the time goes:
time: 1530 us
  waiting for transfers between devices  1190 us (78%)
  blocking collectives  305 us (20%)
    unnamed x5, waiting for transfers between devices  812 us
    psum x1, waiting for transfers between devices, on_device(): lax.psum(enc_half, 'tok').astype(jnp.float32)  301 us
    all_gather x1, blocking collectives, on_device(): gathered = lax.all_gather(source, 'feat', axis=0, tiled=True)  149 us
    all_gather x1, blocking collectives, on_device(): signal_all = lax.all_gather(signal, 'feat', axis=0, tiled=True)  117 us
    all_gather x1, waiting for transfers between devices, on_device(): full_dec = lax.all_gather(dec_weight, 'tok', axis=1, tiled=True)  75.7 us
    psum x1, blocking collectives, on_device(): lax.psum(bias_part, 'tok').astype(jnp.float32)  39.5 us
  transfers between devices with their start and end apart: 4, of which 3 were waited for; matrix products, arithmetic and copies ran while one was open for 0% of the time, Pallas kernels for 0%

commit v1 on v0

--- a/solution.py
+++ b/solution.py
@@ -47,7 +47,7 @@
     enc_half = enc_part.astype(jnp.bfloat16)
     dec_half = dec_part.astype(jnp.bfloat16)
     enc_summed, dec_summed, bias_summed = (
-        lax.psum(enc_half, "tok").astype(jnp.float32),
+        jnp.sum(lax.all_gather(enc_half, axis_name="tok"), 0).astype(jnp.float32),
         lax.psum(dec_half, "tok").astype(jnp.float32),
         lax.psum(bias_part, "tok").astype(jnp.float32),
     )

time: 1530 us -> 1880 us (1.23)
  the two profiles are of different devices: /device:TPU:14 before, /device:TPU:6 now
where the time goes in v1:
time: 1880 us
  waiting for transfers between devices  1520 us (81%)
  blocking collectives  304 us (16%)
    unnamed x6, waiting for transfers between devices  816 us
    all_gather x1, waiting for transfers between devices, on_device(): lax.all_gather(enc_half, axis_name='tok')  420 us
    psum x1, waiting for transfers between devices, on_device(): lax.psum(dec_half, 'tok').astype(jnp.float32)  212 us
    all_gather x1, blocking collectives, on_device(): gathered = lax.all_gather(source, 'feat', axis=0, tiled=True)  148 us
    all_gather x1, blocking collectives, on_device(): signal_all = lax.all_gather(signal, 'feat', axis=0, tiled=True)  120 us
    all_gather x1, waiting for transfers between devices, on_device(): full_dec = lax.all_gather(dec_weight, 'tok', axis=1, tiled=True)  74.9 us
  transfers between devices with their start and end apart: 5, of which 4 were waited for; matrix products, arithmetic and copies ran while one was open for 2% of the time, Pallas kernels for 0%

profile of v1, /device:TPU:6, one launch (start us, length us, event | category | flops | bytes accessed | tf_op | source)
XLA Modules:
  0.0 1883.4 jit_solution(17829285295520499153)
XLA Ops:
  7.2 0.0 copy-start
  7.2 0.0 copy-start.2
  7.2 0.0 all-gather.7.cloned.1.call-start
  7.2 0.7 all-gather.7.cloned.1.call-update
  7.9 0.0 all-gather.9.cloned.1.call-start
  8.0 0.7 all-gather.9.cloned.1.call-update
  8.7 0.0 all-reduce.6.cloned.1.call-start
  8.7 147.5 %all-gather.1 = bf16[64,2,3584]{2,1,0:T(2,128)(2,1)S(1)} all-gather(bf16[1,2,3584]{2,1,0:T(2,128)(2,1)} %bitcast.22), channel_id=1, replica_groups=mesh['feat'=64,'tok'=8] {'feat'}, dimensions={0}, use_global_device_ids=true | all-gather | bytes 931840 | tf_op jit(solution)/shard_map/all_gather | solution.py:12
  156.2 0.3 reshape.11
  156.6 0.0 all-gather.7.cloned.1.call-done
  156.6 0.0 copy-done
  156.6 0.0 copy-done.2
  156.6 1.9 fusion.2
  158.6 74.9 %all-gather.9.cloned.1.call-done = bf16[256,3584]{0,1:T(8,128)(2,1)} async-done(((bf16[256,448]{0,1:T(8,128)(2,1)}), bf16[256,3584]{0,1:T(8,128)(2,1)}) %all-gather.9.cloned.1.call-update) | async-done | bytes 1835024 | tf_op jit(solution)/shard_map/all_gather | solution.py:24
  233.5 3.5 fusion.6
  236.9 0.0 copy-start.1
  236.9 0.0 all-reduce.6.cloned.1.call-update
  236.9 0.0 all-gather.11.cloned.1.call-start
  237.0 1.3 dynamic-slice
  238.9 814.5 %all-reduce.6.cloned.1.call-done = f32[128,3584]{1,0:T(8,128)} async-done(((f32[128,3584]{1,0:T(8,128)}), f32[128,3584]{1,0:T(8,128)}) %all-reduce.6.cloned.1.call-update) | async-done | bytes 1835024
  1053.5 0.0 copy-done.1
  1053.5 1.5 fusion.4
  1055.0 120.4 %all-gather.2 = bf16[64,2,3584]{2,1,0:T(2,128)(2,1)S(1)} all-gather(bf16[1,2,3584]{2,1,0:T(2,128)(2,1)S(1)} %get-tuple-element.8), channel_id=1, replica_groups=mesh['feat'=64,'tok'=8] {'feat'}, dimensions={0}, use_global_device_ids=true | all-gather | bytes 931840 | tf_op jit(solution)/shard_map/all_gather | solution.py:34
  1175.4 0.3 reshape.13
  1175.8 1.9 fusion.5
  1177.7 1.9 fusion
  1179.6 0.0 all-gather.11.cloned.1.call-update
  1179.6 0.0 all-reduce.4.cloned.1.call-start
  1179.7 1.9 convolution_convert_fusion
  1181.6 0.0 all-reduce.4.cloned.1.call-update
  1181.6 36.2 %psum.14 = bf16[256]{0:T(256)(128)(2,1)S(1)} all-reduce(bf16[256]{0:T(256)(128)(2,1)S(1)} %get-tuple-element.10), channel_id=1, replica_groups=mesh['feat'=64,'tok'=8] {'tok'}, use_global_device_ids=true, to_apply=%region_3.0 | all-reduce | flops 256 | bytes 1024 | tf_op jit(solution)/shard_map/psum | solution.py:52
  1217.8 0.6 convert_element_type.44
  1218.4 420.0 %all-gather.11.cloned.1.call-done = bf16[28672,256]{0,1:T(8,128)(2,1)} async-done(((bf16[3584,256]{0,1:T(8,128)(2,1)}), bf16[28672,256]{0,1:T(8,128)(2,1)}) %all-gather.11.cloned.1.call-update) | async-done | bytes 14680080 | tf_op jit(solution)/shard_map/all_gather | solution.py:50
  1638.4 10.8 copy.11
  1649.2 11.0 bitcast_reduce_fusion
  1660.2 2.3 copy.10
  1662.5 211.5 %all-reduce.4.cloned.1.call-done = bf16[256,3584]{1,0:T(8,128)(2,1)} async-done(((bf16[256,3584]{1,0:T(8,128)(2,1)}), bf16[256,3584]{1,0:T(8,128)(2,1)}) %all-reduce.4.cloned.1.call-update) | async-done | bytes 1835024 | tf_op jit(solution)/shard_map/psum | solution.py:51
  1874.0 2.8 copy.14
Async XLA Ops:
  7.2 149.5 %copy-start = (s32[128,256]{1,0:T(8,128)S(1)}, s32[128,256]{1,0:T(8,128)}, u32[]{:S(2)}) copy-start(s32[128,256]{1,0:T(8,128)} %param.11) | copy-start | bytes 393220
  7.2 149.5 %copy-start.2 = (f32[256]{0:T(256)S(1)}, f32[256]{0:T(256)}, u32[]{:S(2)}) copy-start(f32[256]{0:T(256)} %param.9) | copy-start | bytes 3076
  7.2 149.4 %all-gather.7.cloned.1.call-start = ((), (), s32[]{:S(2)}) async-start(), calls=%async_computation | async-start | bytes 2064384 | tf_op jit(solution)/shard_map/all_gather | solution.py:17
  7.9 225.5 %all-gather.9.cloned.1.call-start = ((), (), s32[]{:S(2)}) async-start(), calls=%async_computation.1 | async-start | bytes 2064384 | tf_op jit(solution)/shard_map/all_gather | solution.py:24
  8.7 1044.8 %all-reduce.6.cloned.1.call-start = ((), (), s32[]{:S(2)}) async-start(), calls=%async_computation.4 | async-start | bytes 3670016
  236.9 816.5 %copy-start.1 = (bf16[2,3584]{1,0:T(2,128)(2,1)S(1)}, bf16[2,3584]{1,0:T(2,128)(2,1)}, u32[]{:S(2)}) copy-start(bf16[2,3584]{1,0:T(2,128)(2,1)} %param.7) | copy-start | bytes 43012
  236.9 1401.5 %all-gather.11.cloned.1.call-start = ((), (), s32[]{:S(2)}) async-start(), calls=%async_computation.3 | async-start | bytes 16515072 | tf_op jit(solution)/shard_map/all_gather | solution.py:50
  1179.6 694.4 %all-reduce.4.cloned.1.call-start = ((), (), s32[]{:S(2)}) async-start(), calls=%async_computation.2 | async-start | bytes 3670016 | tf_op jit(solution)/shard_map/psum | solution.py:51
Sparse Core Ops, SparseCore 0:
  11.2 117.5 all-gather.6
  132.0 101.3 all-gather.8
  237.1 816.3 all-reduce.5
  1179.7 458.6 all-gather.10
  1641.5 232.4 all-reduce.3
